TPU v7x, 256 devices: a whole 4x4x8 slice. The times are simulated.
256 devices in a mesh: section: 8 (over x, y_hi), replica: 4 (over y_lo, core), tensor: 8 (over z).
Axes of the slice: x: 4, y: 4 (y_hi: 2, y_lo: 2; y = y_hi * 2 + y_lo), z: 8, core: 2. Of those that a mesh axis runs over, the one named last changes fastest.
Arguments:
- up_qkv: bfloat16 [8, 4, 1024, 12288], P('section', 'replica', 'tensor'), may hold values from -8 to 8
- down_qk: bfloat16 [8, 4, 512, 2, 8192], P('section', 'replica', 'tensor'), may hold values from -8 to 8
- down_values: bfloat16 [8, 4, 512, 2, 4096], P('section', 'replica', 'tensor'), may hold values from -6 to 6
Outputs:
- up_out: bfloat16 [8, 4, 1024, 4096], P('section', 'replica', 'tensor')
- down_out: bfloat16 [8, 4, 512, 2, 4096], P('section', 'replica', 'tensor')
All inputs are finite; a program needn't handle non-finite values.
Results may differ from a plain program's by a relative error of at most 0.011.
Values may be sent and summed in bfloat16 or wider, within the bound.
A program may use at most 64 MiB of HBM per device.

v0:
```python
import jax
import jax.numpy as jnp
from jax import lax
from jax.sharding import PartitionSpec as P

HEADS = 32
HD = 128
SEQ = 1024


def passed_along(array, axis, by):
    peers = lax.axis_size(axis)
    pairs = [(i, i + by) for i in range(peers) if 0 <= i + by < peers]
    return lax.ppermute(array, axis, pairs)


def partner(value, axis, distance):
    mask = 2**distance
    pairs = [(source, source ^ mask) for source in range(lax.axis_size(axis))]
    return lax.ppermute(value, axis, pairs)


def attend(queries, key_rows, values, query_pos, key_pos):
    length = queries.shape[0]
    block_rows = min(512, length)
    block_count = length // block_rows
    score_scale = 1.0 / queries.shape[2] ** 0.5

    def one_block(block_index):
        first_row = block_index * block_rows
        query_block = lax.dynamic_slice_in_dim(queries, first_row, block_rows, 0)
        block_pos = lax.dynamic_slice_in_dim(query_pos, first_row, block_rows, 0)
        scores = (
            jnp.einsum("qhd,khd->hqk", query_block, key_rows, preferred_element_type=jnp.float32)
            * score_scale
        )
        allowed = key_pos[None, None, :] <= block_pos[None, :, None]
        scores = jnp.where(allowed, scores, jnp.float32(-1e30))
        row_peak = jnp.max(scores, axis=2, keepdims=True)
        expsum = jnp.exp(scores - row_peak)
        weights = (expsum / jnp.sum(expsum, axis=2, keepdims=True)).astype(jnp.bfloat16)
        return jnp.einsum(
            "hqk,khd->qhd", weights, values, preferred_element_type=jnp.float32
        ).astype(jnp.bfloat16)

    blocks = lax.map(one_block, jnp.arange(block_count, dtype=jnp.int32))
    return blocks.reshape(length, queries.shape[1], queries.shape[2])


def attend_stacked(stacked, positions):
    return attend(stacked[:, 0], stacked[:, 1], stacked[:, 2], positions, positions)


def pick_seq(stacked_in, selector):
    return lax.dynamic_index_in_dim(stacked_in, selector, 1, keepdims=False)


def by_parity(own_part, other_part, parity):
    first = jnp.stack([own_part, other_part], axis=1)
    second = jnp.stack([other_part, own_part], axis=1)
    return jnp.where(parity == 0, first, second)


def mixed_stack(query_keys, own_values, own_part, other_part, parity):
    carried_down = by_parity(own_part, other_part, parity)
    mixed_values = (own_values.astype(jnp.float32) + carried_down.astype(jnp.float32)).astype(
        jnp.bfloat16
    )
    return jnp.concatenate(
        [query_keys, mixed_values.reshape(query_keys.shape[0], 2, 1, HEADS, HD)], axis=2
    )


def per_device(up_qkv, down_qk, down_values):
    local_rows = up_qkv.shape[2]
    half_rows = down_qk.shape[2]
    model_width = HEADS * HD
    parity = lax.axis_index("replica") % 2
    opposite = 1 - parity
    natural_pos = jnp.arange(SEQ, dtype=jnp.int32)
    upper_parts = up_qkv.reshape(local_rows, 3, HEADS, HD)
    by_heads = lax.all_to_all(upper_parts, "tensor", split_axis=2, concat_axis=0, tiled=True)
    up_heads_out = attend_stacked(by_heads, natural_pos)
    up_tokens = lax.all_to_all(up_heads_out, "tensor", split_axis=0, concat_axis=1, tiled=True)
    up_out = up_tokens.reshape(1, 1, local_rows, model_width)
    carried = passed_along(up_out, "section", 1)
    query_keys = down_qk.reshape(half_rows, 2, 2, HEADS, HD)
    own_values = down_values.reshape(half_rows, 2, model_width)
    carried_pairs = carried.reshape(half_rows, 2, model_width)
    carried_back = partner(pick_seq(carried_pairs, opposite), "replica", 0)
    stacked = mixed_stack(
        query_keys, own_values, pick_seq(carried_pairs, parity), carried_back, parity
    )
    groups = lax.axis_size("replica") // 2
    half_len = SEQ // 2
    wide_pos = 2 * (natural_pos % half_len) + natural_pos // half_len
    gathered = lax.all_to_all(
        stacked, ("replica", "tensor"), split_axis=3, concat_axis=0, tiled=True
    )
    item_count = gathered.shape[1]
    heads_here = gathered.shape[3]
    grouped = gathered.reshape(groups, SEQ, item_count, 3, heads_here, HD)

    def one_group(group_part):
        queries = group_part[:, :, 0].reshape(SEQ, item_count * heads_here, HD)
        key_rows = group_part[:, :, 1].reshape(SEQ, item_count * heads_here, HD)
        values = group_part[:, :, 2].reshape(SEQ, item_count * heads_here, HD)
        outcome = attend(queries, key_rows, values, wide_pos, wide_pos)
        return outcome.reshape(SEQ, item_count, heads_here, HD)

    results = lax.map(one_group, grouped).reshape(groups * SEQ, item_count, heads_here, HD)
    down_tokens = lax.all_to_all(
        results, ("replica", "tensor"), split_axis=0, concat_axis=2, tiled=True
    ).reshape(half_rows, 2, model_width)
    down_out = down_tokens.reshape(1, 1, half_rows, 2, model_width)
    return (up_out, down_out)


def solution(mesh):
    placed = (
        P("section", "replica", "tensor", None),
        P("section", "replica", "tensor", None, None),
        P("section", "replica", "tensor", None, None),
    )
    return jax.shard_map(
        per_device,
        mesh=mesh,
        in_specs=placed,
        out_specs=(
            P("section", "replica", "tensor", None),
            P("section", "replica", "tensor", None, None),
        ),
        check_vma=False,
    )
```

profile of v0, /device:TPU:225, one launch (start us, length us, event | category | flops | bytes accessed | tf_op | source)
XLA Modules:
  0.0 353.2 jit_solution(18139924611987749585)
XLA Ops:
  0.6 3.5 copy.54
  6.0 5.3 %all-to-all-start = ((bf16[128,3,32,128]{0,3,1,2:T(8,128)(2,1)}), bf16[128,3,32,128]{0,3,1,2:T(8,128)(2,1)S(1)}, u32[]{:S(2)}, u32[]{:S(2)}) async-start(bf16[128,3,32,128]{0,3,1,2:T(8,128)(2,1)} %copy.55), calls=%async_computation | async-start | bytes 6291456 | tf_op jit(solution)/shard_map/all_to_all | solution.py:82
  11.3 64.9 %all-to-all-done = bf16[128,3,32,128]{0,3,1,2:T(8,128)(2,1)S(1)} async-done(((bf16[128,3,32,128]{0,3,1,2:T(8,128)(2,1)}), bf16[128,3,32,128]{0,3,1,2:T(8,128)(2,1)S(1)}, u32[]{:S(2)}, u32[]{:S(2)}) %all-to-all-start) | async-done | bytes 3145760 | tf_op jit(solution)/shard_map/all_to_all | solution.py:82
  79.0 3.5 %slice_bitcast_fusion.3 = (bf16[1024,4,128]{2,0,1:T(8,128)(2,1)S(1)}, bf16[1024,4,128]{2,0,1:T(8,128)(2,1)}, bf16[1024,4,128]{2,0,1:T(8,128)(2,1)}) fusion(bf16[1024,3,4,128]{3,0,2,1:T(8,128)(2,1)} %bitcast.104), kind=kLoop, calls=%fused_computation.65 | loop fusion | bytes 6291456 | tf_op jit(solution)/shard_map/squeeze | solution.py:51
  82.6 28.3 %while.36 = (s32[]{:T(128)}, bf16[2,512,4,128]{3,1,0,2:T(8,128)(2,1)S(1)}, s32[1024]{0:T(1024)S(1)}, s32[2]{0:T(128)S(1)}, bf16[1024,4,128]{2,0,1:T(8,128)(2,1)}...) while((s32[]{:T(128)}, ...), condition=%wide.region_3.4_spmd.clone, body=%wide.region_0.3_spmd.clone.sunk | while | flops 1087112192 | bytes 20998332 | solution.py:46
  84.3 7.7 %fusion.91 = (f32[4,512]{1,0:T(4,128)S(1)}, f32[4,512,1024]{2,1,0:T(8,128)}) fusion(pred[512,1024]{1,0:T(8,128)(4,1)S(1)} %broadcast_compare_fusion.4, bf16[1024,4,128]{2,0,1:T(8,128)(2,1)} %get-tuple-element.427, bf16[1024,4,128]{2,0,1:T(8,128)(2,1)} %get-tuple-element.426, s32[]{:T(128)S(6)} %select_n.118), kind=kOutput, calls=%fused_computation.72.clone.1 | convolution fusion | flops 545260544 | bytes 10493956 | tf_op jit(solution)/shard_map/while/body/eval_jaxpr/sub | solution.py:40
  91.9 4.8 %fusion.92 = bf16[2,512,4,128]{3,1,0,2:T(8,128)(2,1)S(1)} fusion(bf16[2,512,4,128]{3,1,0,2:T(8,128)(2,1)S(1)} %get-tuple-element.412, s32[]{:T(128)S(6)} %copy.112, bf16[1024,4,128]{2,0,1:T(8,128)(2,1)S(1)} %get-tuple-element.428, f32[4,512,1024]{2,1,0:T(8,128)} %get-tuple-element.348, f32[4,512]{1,0:T(4,128)S(1)} %get-tuple-element.349), kind=kOutput, calls=%fused_computation.12.clone.1 | convolution fusion | flops 541327360 | bytes 9969668 | tf_op jit(solution)/shard_map/while/body/eval_jaxpr/hqk,khd->qhd/dot_general | solution.py:42
  98.4 7.6 %fusion.91 = (f32[4,512]{1,0:T(4,128)S(1)}, f32[4,512,1024]{2,1,0:T(8,128)}) fusion(pred[512,1024]{1,0:T(8,128)(4,1)S(1)} %broadcast_compare_fusion.4, bf16[1024,4,128]{2,0,1:T(8,128)(2,1)} %get-tuple-element.427, bf16[1024,4,128]{2,0,1:T(8,128)(2,1)} %get-tuple-element.426, s32[]{:T(128)S(6)} %select_n.118), kind=kOutput, calls=%fused_computation.72.clone.1 | convolution fusion | flops 545260544 | bytes 10493956 | tf_op jit(solution)/shard_map/while/body/eval_jaxpr/sub | solution.py:40
  106.1 4.8 %fusion.92 = bf16[2,512,4,128]{3,1,0,2:T(8,128)(2,1)S(1)} fusion(bf16[2,512,4,128]{3,1,0,2:T(8,128)(2,1)S(1)} %get-tuple-element.412, s32[]{:T(128)S(6)} %copy.112, bf16[1024,4,128]{2,0,1:T(8,128)(2,1)S(1)} %get-tuple-element.428, f32[4,512,1024]{2,1,0:T(8,128)} %get-tuple-element.348, f32[4,512]{1,0:T(4,128)S(1)} %get-tuple-element.349), kind=kOutput, calls=%fused_computation.12.clone.1 | convolution fusion | flops 541327360 | bytes 9969668 | tf_op jit(solution)/shard_map/while/body/eval_jaxpr/hqk,khd->qhd/dot_general | solution.py:42
  111.7 34.5 %all_to_all.63 = bf16[1024,4,128]{2,1,0:T(4,128)(2,1)S(1)} all-to-all(bf16[1024,4,128]{2,1,0:T(4,128)(2,1)S(1)} %copy.59), channel_id=1, replica_groups=mesh['section'=8,'replica'=4,'tensor'=8] {'tensor'}, dimensions={0} | all-to-all | bytes 2097152 | tf_op jit(solution)/shard_map/all_to_all | solution.py:84
  147.0 5.0 %collective-permute-start = (bf16[1,1,128,4096]{2,3,1,0:T(8,128)(2,1)S(1)}, bf16[1,1,128,4096]{2,3,1,0:T(8,128)(2,1)S(1)}, u32[]{:S(2)}, u32[]{:S(2)}) collective-permute-start(bf16[1,1,128,4096]{2,3,1,0:T(8,128)(2,1)S(1)} %bitcast.106), channel_id=1, source_target_pairs={{0,32},{32,64},{64,96},{96,128},{128,160},{160,192},{192,224},{1,3... | collective-permute-start | bytes 3145736 | tf_op jit(solution)/shard_map/ppermute | solution.py:14
  152.0 19.8 %collective-permute-done = bf16[1,1,128,4096]{2,3,1,0:T(8,128)(2,1)S(1)} collective-permute-done((bf16[1,1,128,4096]{2,3,1,0:T(8,128)(2,1)S(1)}, bf16[1,1,128,4096]{2,3,1,0:T(8,128)(2,1)S(1)}, u32[]{:S(2)}, u32[]{:S(2)}) %collective-permute-start) | collective-permute-done | bytes 1048608 | tf_op jit(solution)/shard_map/ppermute | solution.py:14
  173.1 4.2 %dynamic-slice_reduce_fusion = (bf16[64,4096]{1,0:T(8,128)(2,1)S(1)}, bf16[64,1,4096]{2,1,0:T(2,128)(2,1)S(1)}) fusion(bf16[64,2,4096]{2,1,0:T(2,128)(2,1)S(1)} %reshape.186, s32[]{:T(128)S(6)} %select_n.62, s32[]{:T(128)S(6)} %select_n.63), kind=kLoop, calls=%fused_computation.69 | loop fusion | bytes 2097160 | tf_op jit(solution)/shard_map/jit(dynamic_index_in_dim)/dynamic_slice | solution.py:55
  177.9 3.3 collective-permute-start.1
  183.0 3.3 reshape.190
  189.0 2.9 copy.67
  191.8 10.0 %all-to-all-start.2 = ((bf16[64,2,3,32,128]{4,0,2,1,3:T(8,128)(2,1)}), bf16[64,2,3,32,128]{4,0,2,1,3:T(8,128)(2,1)S(1)}, u32[]{:S(2)}, u32[]{:S(2)}) async-start(bf16[64,2,3,32,128]{4,0,2,1,3:T(8,128)(2,1)} %copy.67), calls=%async_computation.2 | async-start | bytes 6291456 | tf_op jit(solution)/shard_map/all_to_all | solution.py:97
  201.9 72.0 %all-to-all-done.2 = bf16[64,2,3,32,128]{4,0,2,1,3:T(8,128)(2,1)S(1)} async-done(((bf16[64,2,3,32,128]{4,0,2,1,3:T(8,128)(2,1)}), bf16[64,2,3,32,128]{4,0,2,1,3:T(8,128)(2,1)S(1)}, u32[]{:S(2)}, u32[]{:S(2)}) %all-to-all-start.2) | async-done | bytes 3145760 | tf_op jit(solution)/shard_map/all_to_all | solution.py:97
  276.5 38.8 %while.38 = (s32[]{:T(128)}, bf16[2,1024,2,1,128]{4,1,0,2,3:T(8,128)(2,1)}, bf16[2,1024,2,3,1,128]{5,1,0,3,2,4:T(8,128)(2,1)}, s32[]{:T(128)}, s32[]{:T(128)}, /...) while((s32[]{:T(128)}, bf16[2,1024,2,1,128]{4,1,0,2,3:T(8,128)(2,1)}, ...), condition=%wide.region_9.10_spmd.clone.clone, body=%wide.region_4.9_spmd.clone.clone.sunk | while | flops 543833088 | bytes 18373008 | solution.py:111
  278.1 16.9 %while.39 = (s32[]{:T(128)}, bf16[2,512,2,128]{3,1,0,2:T(8,128)(2,1)S(1)}, s32[1024]{0:T(1024)S(1)}, s32[2]{0:T(128)S(1)}, bf16[1024,2,128]{2,0,1:T(8,128)(2,1)S...) while((s32[]{:T(128)}, ...), condition=%wide.region_8.8_spmd.clone, body=%wide.region_5.7_spmd.clone.sunk | while | flops 543818752 | bytes 11028667 | solution.py:46
  280.0 3.6 %fusion.97 = (f32[2,512]{1,0:T(2,128)S(1)}, f32[2,512,1024]{2,1,0:T(8,128)}) fusion(pred[512,1024]{1,0:T(8,128)(4,1)S(1)} %broadcast_compare_fusion.5, bf16[1024,2,128]{2,0,1:T(8,128)(2,1)S(1)} %get-tuple-element.394, bf16[1024,2,128]{2,0,1:T(8,128)(2,1)S(1)} %get-tuple-element.393, s32[]{:T(128)S(6)} %select_n.122), kind=kOutput, calls=%fused_computation.73.clone.1 | convolution fusion | flops 272630784 | bytes 5509124 | tf_op jit(solution)/shard_map/while/body/eval_jaxpr/while/body/eval_jaxpr/sub | solution.py:40
  283.6 3.0 fusion.98
  288.4 3.6 %fusion.97 = (f32[2,512]{1,0:T(2,128)S(1)}, f32[2,512,1024]{2,1,0:T(8,128)}) fusion(pred[512,1024]{1,0:T(8,128)(4,1)S(1)} %broadcast_compare_fusion.5, bf16[1024,2,128]{2,0,1:T(8,128)(2,1)S(1)} %get-tuple-element.394, bf16[1024,2,128]{2,0,1:T(8,128)(2,1)S(1)} %get-tuple-element.393, s32[]{:T(128)S(6)} %select_n.122), kind=kOutput, calls=%fused_computation.73.clone.1 | convolution fusion | flops 272630784 | bytes 5509124 | tf_op jit(solution)/shard_map/while/body/eval_jaxpr/while/body/eval_jaxpr/sub | solution.py:40
  292.0 3.0 fusion.98
  297.5 16.9 %while.39 = (s32[]{:T(128)}, bf16[2,512,2,128]{3,1,0,2:T(8,128)(2,1)S(1)}, s32[1024]{0:T(1024)S(1)}, s32[2]{0:T(128)S(1)}, bf16[1024,2,128]{2,0,1:T(8,128)(2,1)S...) while((s32[]{:T(128)}, ...), condition=%wide.region_8.8_spmd.clone, body=%wide.region_5.7_spmd.clone.sunk | while | flops 543818752 | bytes 11028667 | solution.py:46
  299.4 3.6 %fusion.97 = (f32[2,512]{1,0:T(2,128)S(1)}, f32[2,512,1024]{2,1,0:T(8,128)}) fusion(pred[512,1024]{1,0:T(8,128)(4,1)S(1)} %broadcast_compare_fusion.5, bf16[1024,2,128]{2,0,1:T(8,128)(2,1)S(1)} %get-tuple-element.394, bf16[1024,2,128]{2,0,1:T(8,128)(2,1)S(1)} %get-tuple-element.393, s32[]{:T(128)S(6)} %select_n.122), kind=kOutput, calls=%fused_computation.73.clone.1 | convolution fusion | flops 272630784 | bytes 5509124 | tf_op jit(solution)/shard_map/while/body/eval_jaxpr/while/body/eval_jaxpr/sub | solution.py:40
  303.0 3.0 fusion.98
  307.8 3.6 %fusion.97 = (f32[2,512]{1,0:T(2,128)S(1)}, f32[2,512,1024]{2,1,0:T(8,128)}) fusion(pred[512,1024]{1,0:T(8,128)(4,1)S(1)} %broadcast_compare_fusion.5, bf16[1024,2,128]{2,0,1:T(8,128)(2,1)S(1)} %get-tuple-element.394, bf16[1024,2,128]{2,0,1:T(8,128)(2,1)S(1)} %get-tuple-element.393, s32[]{:T(128)S(6)} %select_n.122), kind=kOutput, calls=%fused_computation.73.clone.1 | convolution fusion | flops 272630784 | bytes 5509124 | tf_op jit(solution)/shard_map/while/body/eval_jaxpr/while/body/eval_jaxpr/sub | solution.py:40
  311.4 3.0 fusion.98
  315.3 3.7 %copy.71 = bf16[2048,2,1,128]{3,1,2,0:T(2,128)(2,1)} copy(bf16[2048,2,1,128]{3,0,1,2:T(8,128)(2,1)} %bitcast.114) | data formatting | bytes 2097152 | tf_op jit(solution)/shard_map/reshape | solution.py:111
  319.0 5.7 %all-to-all-start.3 = ((bf16[2048,2,1,128]{3,1,2,0:T(2,128)(2,1)}), bf16[2048,2,1,128]{3,1,2,0:T(2,128)(2,1)S(1)}, u32[]{:S(2)}, u32[]{:S(2)}) async-start(bf16[2048,2,1,128]{3,1,2,0:T(2,128)(2,1)} %copy.71), calls=%async_computation.3 | async-start | bytes 2097152 | tf_op jit(solution)/shard_map/all_to_all | solution.py:112
  326.1 25.2 %all-to-all-done.3 = bf16[2048,2,1,128]{3,1,2,0:T(2,128)(2,1)S(1)} async-done(((bf16[2048,2,1,128]{3,1,2,0:T(2,128)(2,1)}), bf16[2048,2,1,128]{3,1,2,0:T(2,128)(2,1)S(1)}, u32[]{:S(2)}, u32[]{:S(2)}) %all-to-all-start.3) | async-done | bytes 1048608 | tf_op jit(solution)/shard_map/all_to_all | solution.py:112
  (63 shorter events, 29.8 us)
Async XLA Ops:
  6.0 70.2 %all-to-all-start = ((bf16[128,3,32,128]{0,3,1,2:T(8,128)(2,1)}), bf16[128,3,32,128]{0,3,1,2:T(8,128)(2,1)S(1)}, u32[]{:S(2)}, u32[]{:S(2)}) async-start(bf16[128,3,32,128]{0,3,1,2:T(8,128)(2,1)} %copy.55), calls=%async_computation | async-start | bytes 6291456 | tf_op jit(solution)/shard_map/all_to_all | solution.py:82
  79.0 3.6 %copy-start.4 = (bf16[2,512,4,128]{3,1,0,2:T(8,128)(2,1)S(1)}, bf16[2,512,4,128]{3,1,0,2:T(8,128)(2,1)}, u32[]{:S(2)}) copy-start(bf16[2,512,4,128]{3,1,0,2:T(8,128)(2,1)} %custom-call.1) | copy-start | bytes 3145732
  147.0 24.9 %copy-start.1 = (bf16[128,8,4,128]{0,3,2,1:T(8,128)(2,1)}, bf16[128,8,4,128]{0,3,2,1:T(8,128)(2,1)S(1)}, u32[]{:S(2)}) copy-start(bf16[128,8,4,128]{0,3,2,1:T(8,128)(2,1)S(1)} %copy.61) | copy-start | bytes 3145732
  147.0 24.9 %collective-permute-start = (bf16[1,1,128,4096]{2,3,1,0:T(8,128)(2,1)S(1)}, bf16[1,1,128,4096]{2,3,1,0:T(8,128)(2,1)S(1)}, u32[]{:S(2)}, u32[]{:S(2)}) collective-permute-start(bf16[1,1,128,4096]{2,3,1,0:T(8,128)(2,1)S(1)} %bitcast.106), channel_id=1, source_target_pairs={{0,32},{32,64},{64,96},{96,128},{128,160},{160,192},{192,224},{1,3... | collective-permute-start | bytes 3145736 | tf_op jit(solution)/shard_map/ppermute | solution.py:14
  173.1 8.1 %copy-start.3 = (bf16[1,1,64,2,4096]{4,3,2,1,0:T(2,128)(2,1)S(1)}, bf16[1,1,64,2,4096]{4,3,2,1,0:T(2,128)(2,1)}, u32[]{:S(2)}) copy-start(bf16[1,1,64,2,4096]{4,3,2,1,0:T(2,128)(2,1)} %param.11) | copy-start | bytes 3145732
  177.9 8.5 %collective-permute-start.1 = (bf16[64,4096]{1,0:T(8,128)(2,1)S(1)}, bf16[64,4096]{1,0:T(8,128)(2,1)}, u32[]{:S(2)}, u32[]{:S(2)}) collective-permute-start(bf16[64,4096]{1,0:T(8,128)(2,1)S(1)} %bitcast.115), channel_id=1, source_target_pairs={{0,8},{8,0},{16,24},{24,16},{1,9},{9,1},{17,25},{25,17},{2,10},{10... | collective-permute-start | bytes 1572872 | tf_op jit(solution)/shard_map/ppermute | solution.py:20
  186.3 1.7 copy-start
  191.8 82.0 %all-to-all-start.2 = ((bf16[64,2,3,32,128]{4,0,2,1,3:T(8,128)(2,1)}), bf16[64,2,3,32,128]{4,0,2,1,3:T(8,128)(2,1)S(1)}, u32[]{:S(2)}, u32[]{:S(2)}) async-start(bf16[64,2,3,32,128]{4,0,2,1,3:T(8,128)(2,1)} %copy.67), calls=%async_computation.2 | async-start | bytes 6291456 | tf_op jit(solution)/shard_map/all_to_all | solution.py:97
  315.3 9.4 %copy-start.2 = (bf16[128,8,4,128]{0,3,2,1:T(8,128)(2,1)S(1)}, bf16[128,8,4,128]{0,3,2,1:T(8,128)(2,1)}, u32[]{:S(2)}) copy-start(bf16[128,8,4,128]{0,3,2,1:T(8,128)(2,1)} %copy-done.1) | copy-start | bytes 3145732
  319.0 32.2 %all-to-all-start.3 = ((bf16[2048,2,1,128]{3,1,2,0:T(2,128)(2,1)}), bf16[2048,2,1,128]{3,1,2,0:T(2,128)(2,1)S(1)}, u32[]{:S(2)}, u32[]{:S(2)}) async-start(bf16[2048,2,1,128]{3,1,2,0:T(2,128)(2,1)} %copy.71), calls=%async_computation.3 | async-start | bytes 2097152 | tf_op jit(solution)/shard_map/all_to_all | solution.py:112
where the time goes:
time: 360 us; the launch traced here: 353 us
  waiting for transfers between devices  182 us (51%)
  matrix products  51.4 us (14%)
  local copies, waits for them, and re-layouts  47.7 us (13%)
  blocking collectives  34.5 us (10%)
  starting transfers between devices  29.4 us (8%)
  loops' own time  4.34 us (1%)
    all_to_all x1, waiting for transfers between devices, per_device(): lax.all_to_all(stacked, ('replica', 'tensor'), split_axis=3, concat_axis=...  72 us
    all_to_all x1, waiting for transfers between devices, per_device(): lax.all_to_all(upper_parts, 'tensor', split_axis=2, concat_axis=0, tiled=...  64.9 us
    all_to_all x1, blocking collectives, per_device(): lax.all_to_all(up_heads_out, 'tensor', split_axis=0, concat_axis=1, tiled...  34.5 us
    sub x6, matrix products, one_block(): expsum = jnp.exp(scores - row_peak)  29.8 us
    all_to_all x1, waiting for transfers between devices, per_device(): lax.all_to_all(results, ('replica', 'tensor'), split_axis=0, concat_axis=...  25.2 us
    dot_general x6, matrix products, one_block(): jnp.einsum('hqk,khd->qhd', weights, values, preferred_element_type=jnp.fl...  21.6 us
    ppermute x1, waiting for transfers between devices, passed_along(): return lax.ppermute(array, axis, pairs)  19.8 us
    all_to_all x1, starting transfers between devices, per_device(): lax.all_to_all(stacked, ('replica', 'tensor'), split_axis=3, concat_axis=...  10 us
  transfers between devices with their start and end apart: 5, of which 4 were waited for; matrix products, arithmetic and copies ran while one was open for 2% of the time, Pallas kernels for 0%

commit v1 on v0

v1 whole, which is shorter than its diff:
```python
import functools
import math

import jax
import jax.numpy as jnp
from jax import lax
from jax.experimental import pallas as pl
from jax.experimental.pallas import tpu as pltpu
from jax.sharding import PartitionSpec as P

HD = 128
QB = 256
LOG2E = 1.4426950408889634


def exchange_kernel(
    sizes,
    up_ref,
    dqk_ref,
    dv_ref,
    upo_ref,
    dno_ref,
    upbuf,
    dnbuf,
    carr,
    upres,
    dnres,
    up_ssem,
    up_rsem,
    dn_ssem,
    dn_rsem,
    uo_ssem,
    uo_rsem,
    do_ssem,
    do_rsem,
    ca_ssem,
    ca_rsem,
    own_sem,
):
    sections, tensors, rows, width = sizes
    half = rows // 2
    seq = tensors * rows
    cols = width // tensors
    heads = cols // HD
    s = lax.axis_index("section")
    r = lax.axis_index("replica")
    z = lax.axis_index("tensor")
    core = lax.rem(r, 2)
    pair = r - core
    distances = sorted(range(1, tensors), key=lambda d: -min(d, tensors - d))

    def at(other_core, other_z):
        return {"replica": pair + other_core, "tensor": other_z}

    def z_at(d):
        return lax.rem(z + d, tensors)

    def lanes(index, size):
        return pl.ds(pl.multiple_of(index * size, size), size)

    def remote(src, dst, ssem, rsem, device):
        return pltpu.make_async_remote_copy(
            src_ref=src,
            dst_ref=dst,
            send_sem=ssem,
            recv_sem=rsem,
            device_id=device,
            device_id_type=pl.DeviceIdType.MESH,
        )

    barrier = pltpu.get_barrier_semaphore()
    for d in range(tensors):
        for flip in range(2):
            if d or flip:
                other = core + flip - 2 * flip * core
                pl.semaphore_signal(
                    barrier, inc=1, device_id=at(other, z_at(d)), device_id_type=pl.DeviceIdType.MESH
                )
    for step in (1, sections - 1):
        pl.semaphore_signal(
            barrier,
            inc=1,
            device_id={"section": lax.rem(s + step, sections)},
            device_id_type=pl.DeviceIdType.MESH,
        )
    pl.semaphore_wait(barrier, 2 * tensors - 1 + 2)

    def up_own(part):
        return pltpu.make_async_copy(
            up_ref.at[:, pl.ds(pl.multiple_of(part * width + z * cols, cols), cols)],
            upbuf.at[part, lanes(z, rows), :],
            own_sem.at[part],
        )

    def up_send(part, d):
        return remote(
            up_ref.at[:, pl.ds(pl.multiple_of(part * width + z_at(d) * cols, cols), cols)],
            upbuf.at[part, lanes(z, rows), :],
            up_ssem.at[part, d],
            up_rsem.at[part, d],
            at(core, z_at(d)),
        )

    def dn_source(part, other_core, other_z):
        if part < 2:
            return dqk_ref.at[other_core, :, pl.ds(pl.multiple_of(part * width + other_z * cols, cols), cols)]
        return dv_ref.at[other_core, :, lanes(other_z, cols)]

    def dn_place(part):
        return dnbuf.at[part, pl.ds(pl.multiple_of(z * rows + core * half, half), half), :]

    def dn_own(part):
        return pltpu.make_async_copy(dn_source(part, core, z), dn_place(part), own_sem.at[3 + part])

    def dn_send(part, flip, d):
        other = core + flip - 2 * flip * core
        return remote(
            dn_source(part, other, z_at(d)),
            dn_place(part),
            dn_ssem.at[part, flip, d],
            dn_rsem.at[part, flip, d],
            at(other, z_at(d)),
        )

    for part in range(3):
        up_own(part).start()
        for d in distances:
            up_send(part, d).start()
    for part in range(3):
        dn_own(part).start()

    dn_targets = [(0, d) for d in distances] + [(1, d) for d in distances] + [(1, 0)]
    for part in range(3):
        for d in distances:
            up_send(part, d).wait_send()
        for flip, d in dn_targets:
            dn_send(part, flip, d).start()

    scale = LOG2E / math.sqrt(HD)

    def attend_head(buf, out, head, position):
        at_head = lanes(head, HD)
        for block in range(seq // QB):
            first = block * QB
            q = buf[0, pl.ds(first, QB), at_head]
            keys = buf[1, pl.ds(first, QB), at_head]
            dims = (((1,), (1,)), ((), ()))
            diag = lax.dot_general(q, keys, dims, preferred_element_type=jnp.float32)
            row = position(lax.broadcasted_iota(jnp.int32, (QB, QB), 0))
            col = position(lax.broadcasted_iota(jnp.int32, (QB, QB), 1))
            diag = jnp.where(col <= row, diag, -1e30)
            peak = jnp.max(diag, axis=1, keepdims=True)
            if first:
                past = lax.dot_general(
                    q, buf[1, pl.ds(0, first), at_head], dims, preferred_element_type=jnp.float32
                )
                peak = jnp.maximum(peak, jnp.max(past, axis=1, keepdims=True))
            weights = jnp.exp2((diag - peak) * scale)
            total = jnp.sum(weights, axis=1, keepdims=True)
            mixed = jnp.dot(
                weights.astype(jnp.bfloat16),
                buf[2, pl.ds(first, QB), at_head],
                preferred_element_type=jnp.float32,
            )
            if first:
                weights = jnp.exp2((past - peak) * scale)
                total += jnp.sum(weights, axis=1, keepdims=True)
                mixed += jnp.dot(
                    weights.astype(jnp.bfloat16),
                    buf[2, pl.ds(0, first), at_head],
                    preferred_element_type=jnp.float32,
                )
            out[pl.ds(first, QB), at_head] = (mixed / total).astype(jnp.bfloat16)

    def natural(index):
        return index

    def parity_order(index):
        inside = lax.rem(index, rows)
        return index - inside + 2 * lax.rem(inside, half) + inside // half

    for part in range(3):
        up_own(part).wait()
        for d in distances:
            up_send(part, d).wait_recv()

    def up_target(head):
        return pl.ds(pl.multiple_of(z * cols + head * HD, HD), HD)

    def uo_own(head):
        return pltpu.make_async_copy(
            upres.at[lanes(z, rows), lanes(head, HD)], upo_ref.at[:, up_target(head)], own_sem.at[6]
        )

    def uo_send(head, d):
        return remote(
            upres.at[lanes(z_at(d), rows), lanes(head, HD)],
            upo_ref.at[:, up_target(head)],
            uo_ssem.at[head, d],
            uo_rsem.at[head, d],
            at(core, z_at(d)),
        )

    def ca_send(head):
        return remote(
            upres.at[:, lanes(head, HD)],
            carr.at[:, lanes(head, HD)],
            ca_ssem.at[head],
            ca_rsem.at[head],
            {"section": lax.rem(s + 1, sections)},
        )

    def up_head(head, carry):
        attend_head(upbuf, upres, head, natural)

        @pl.when(s < sections - 1)
        def _():
            ca_send(head).start()

        for d in distances:
            uo_send(head, d).start()
        own = uo_own(head)
        own.start()
        own.wait()
        return carry

    lax.fori_loop(0, heads, up_head, 0)

    for part in range(3):
        dn_own(part).wait()
        for flip, d in dn_targets:
            dn_send(part, flip, d).wait_recv()

    @pl.when(s > 0)
    def _():
        for head in range(heads):
            ca_send(head).wait_recv()

    @pl.when(s == 0)
    def _():
        carr[...] = jnp.zeros_like(carr)

    row = lax.broadcasted_iota(jnp.int32, (rows, rows), 0)
    col = lax.broadcasted_iota(jnp.int32, (rows, rows), 1)
    reorder = jnp.where(col == parity_order(row), 1.0, 0.0).astype(jnp.bfloat16)

    def mix(block, carry):
        here = lanes(block, rows)
        moved = jnp.dot(reorder, carr[here, :], preferred_element_type=jnp.float32)
        dnbuf[2, here, :] = (dnbuf[2, here, :].astype(jnp.float32) + moved).astype(jnp.bfloat16)
        return carry

    lax.fori_loop(0, tensors, mix, 0)

    def do_source(other_core, other_z, head):
        return dnres.at[
            pl.ds(pl.multiple_of(other_z * rows + other_core * half, half), half), lanes(head, HD)
        ]

    def do_own(head):
        return pltpu.make_async_copy(
            do_source(core, z, head), dno_ref.at[core, :, up_target(head)], own_sem.at[7]
        )

    def do_send(head, flip, d):
        other = core + flip - 2 * flip * core
        return remote(
            do_source(other, z_at(d), head),
            dno_ref.at[core, :, up_target(head)],
            do_ssem.at[head, flip, d],
            do_rsem.at[head, flip, d],
            at(other, z_at(d)),
        )

    def do_arrival(head, flip, d):
        other = core + flip - 2 * flip * core
        return remote(
            do_source(other, z_at(d), head),
            dno_ref.at[other, :, up_target(head)],
            do_ssem.at[head, flip, d],
            do_rsem.at[head, flip, d],
            at(other, z_at(d)),
        )

    def dn_head(head, carry):
        attend_head(dnbuf, dnres, head, parity_order)
        for flip, d in dn_targets:
            do_send(head, flip, d).start()
        own = do_own(head)
        own.start()
        own.wait()
        return carry

    lax.fori_loop(0, heads, dn_head, 0)

    for part in range(3):
        for flip, d in dn_targets:
            dn_send(part, flip, d).wait_send()

    def finish(head, carry):
        for d in distances:
            uo_send(head, d).wait()
        for flip, d in dn_targets:
            do_send(head, flip, d).wait_send()
            do_arrival(head, flip, d).wait_recv()

        @pl.when(s < sections - 1)
        def _():
            ca_send(head).wait_send()

        return carry

    lax.fori_loop(0, heads, finish, 0)


def per_device(mesh_sizes, up_qkv, down_qk, down_values):
    sections, tensors = mesh_sizes
    rows = up_qkv.shape[2]
    width = up_qkv.shape[3] // 3
    half = rows // 2
    seq = tensors * rows
    cols = width // tensors
    heads = cols // HD
    up = up_qkv.reshape(rows, 3 * width)
    dqk = jnp.swapaxes(down_qk.reshape(half, 2, 2 * width), 0, 1)
    dv = jnp.swapaxes(down_values.reshape(half, 2, width), 0, 1)
    hbm = pl.BlockSpec(memory_space=pl.ANY)
    dma = pltpu.SemaphoreType.DMA
    up_out, down = pl.pallas_call(
        functools.partial(exchange_kernel, (sections, tensors, rows, width)),
        name="relay",
        out_shape=(
            jax.ShapeDtypeStruct((rows, width), jnp.bfloat16),
            jax.ShapeDtypeStruct((2, half, width), jnp.bfloat16),
        ),
        in_specs=[hbm, hbm, hbm],
        out_specs=(hbm, hbm),
        scratch_shapes=[
            pltpu.VMEM((3, seq, cols), jnp.bfloat16),
            pltpu.VMEM((3, seq, cols), jnp.bfloat16),
            pltpu.VMEM((seq, cols), jnp.bfloat16),
            pltpu.VMEM((seq, cols), jnp.bfloat16),
            pltpu.VMEM((seq, cols), jnp.bfloat16),
            dma((3, tensors)),
            dma((3, tensors)),
            dma((3, 2, tensors)),
            dma((3, 2, tensors)),
            dma((heads, tensors)),
            dma((heads, tensors)),
            dma((heads, 2, tensors)),
            dma((heads, 2, tensors)),
            dma((heads,)),
            dma((heads,)),
            dma((8,)),
        ],
        compiler_params=pltpu.CompilerParams(
            collective_id=0, has_side_effects=True, vmem_limit_bytes=48 * 1024 * 1024
        ),
    )(up, dqk, dv)
    down_out = jnp.swapaxes(down, 0, 1)
    return (
        up_out.reshape(1, 1, rows, width),
        down_out.reshape(1, 1, half, 2, width),
    )


def solution(mesh):
    placed = (
        P("section", "replica", "tensor", None),
        P("section", "replica", "tensor", None, None),
        P("section", "replica", "tensor", None, None),
    )
    sizes = (mesh.shape["section"], mesh.shape["tensor"])
    return jax.shard_map(
        functools.partial(per_device, sizes),
        mesh=mesh,
        in_specs=placed,
        out_specs=(placed[0], placed[1]),
        check_vma=False,
    )
```

time: 360 us -> 203 us (0.56)
  the two profiles are of different devices: /device:TPU:225 before, /device:TPU:1 now
where the time goes in v1:
time: 203 us
  Pallas kernels  196 us (97%)
  local copies, waits for them, and re-layouts  6.15 us (3%)
    pallas_call x1, Pallas kernels, per_device(): pl.pallas_call(functools.partial(exchange_kernel, (sections, tensors, row...  196 us
    unnamed x6, local copies, waits for them, and re-layouts  6.15 us

profile of v1, /device:TPU:1, one launch (start us, length us, event | category | flops | bytes accessed | tf_op | source)
XLA Modules:
  0.0 202.9 jit_solution(10403760693650350329)
XLA Ops:
  0.6 0.0 copy-start
  0.6 2.0 copy.11
  2.6 0.0 copy-done
  2.6 1.2 copy.10
  3.8 196.1 %relay.1 = (bf16[128,4096]{1,0:T(8,128)(2,1)S(1)}, bf16[2,64,4096]{2,1,0:T(8,128)(2,1)S(1)}) custom-call(bf16[128,12288]{1,0:T(8,128)(2,1)} %bitcast.19, bf16[2,64,8192]{2,1,0:T(8,128)(2,1)S(1)} %bitcast.15, bf16[2,64,4096]{2,1,0:T(8,128)(2,1)S(1)} %bitcast.16), custom_call_target="tpu_custom_call" | custom-call | tf_op jit(solution)/shard_map/relay/pallas_call | solution.py:329
  199.9 2.1 %copy.7 = bf16[1,1,64,2,4096]{4,3,2,1,0:T(2,128)(2,1)} copy(bf16[1,1,64,2,4096]{4,2,3,1,0:T(8,128)(2,1)S(1)} %bitcast.18) | data formatting | bytes 2097152
  201.9 1.0 copy.13
Async XLA Ops:
  0.6 2.0 copy-start

commit v2 on v0

v2 whole, which is shorter than its diff:
```python
import functools
import math

import jax
import jax.numpy as jnp
from jax import lax
from jax.experimental import pallas as pl
from jax.experimental.pallas import tpu as pltpu
from jax.sharding import PartitionSpec as P

HD = 128
ROWS = 128
NOTE = 16
RING = 8
LOG2E = 1.4426950408889634
MESH = pl.DeviceIdType.MESH

GROUPS = (
    (
        {0: (3, 1), 1: (4, 0), 2: (0, 2), 3: (0, 1), 5: (1, 0), 6: (0, 1)},
        {2: 1, 3: 5, 4: 5, 5: 4, 6: 4, 7: 4},
    ),
    (
        {0: (2, 1), 1: (3, 0), 2: (4, 0), 3: (0, 2), 4: (0, 1), 6: (1, 0)},
        {2: 1, 3: 0, 4: 6, 5: 6, 6: 5, 7: 5},
    ),
    (
        {0: (0, 3), 1: (0, 2), 2: (0, 1), 3: (1, 0), 4: (2, 0), 5: (0, 2), 6: (0, 1)},
        {4: 3, 5: 3, 6: 3, 7: 2},
    ),
    (
        {0: (0, 2), 1: (0, 1), 2: (1, 0), 3: (2, 0), 4: (3, 0), 5: (0, 2), 6: (0, 1)},
        {3: 2, 4: 2, 5: 2, 6: 1, 7: 1},
    ),
)


class Plan:
    def __init__(self, reach, visits, load):
        arcs = {}
        for j in range(RING):
            down, up = reach.get(j, (0, 0))
            arcs[j] = {(j + h) % RING for h in range(1, up + 1)} | {(j - h) % RING for h in range(1, down + 1)}
        needed = {j: set() for j in range(RING)}
        home = {i: [i] for i in range(RING)}
        away = {i: [] for i in range(RING)}
        loose = []
        for i in range(RING):
            load[i] += 1
            for j in range(i):
                spot = visits.get(i)
                here = i in arcs[j]
                there = spot is not None and (spot in arcs[j] or spot == j)
                assert here or there, (i, j)
                if here and there:
                    loose.append((i, j))
                elif here:
                    home[i].append(j)
                    needed[j].add(i)
                    load[i] += 1
                else:
                    away[i].append(j)
                    load[spot] += 1
                    if spot != j:
                        needed[j].add(spot)
        for i, j in loose:
            spot = visits[i]
            extra_home = 0 if i in needed[j] else 8
            extra_away = 0 if spot == j or spot in needed[j] else 8
            if load[i] + extra_home <= load[spot] + extra_away:
                home[i].append(j)
                needed[j].add(i)
                load[i] += 1
            else:
                away[i].append(j)
                load[spot] += 1
                if spot != j:
                    needed[j].add(spot)
        self.home = {i: sorted(home[i]) for i in home}
        self.away = {i: sorted(away[i]) for i in away}
        self.visits = {i: n for i, n in visits.items() if away[i]}
        self.slots = {n: [j for j in range(RING) if n in needed[j]] for n in range(RING)}
        self.guests = {n: [i for i in range(RING) if self.visits.get(i) == n] for n in range(RING)}
        self.edges = {n: [] for n in range(RING)}
        for j in range(RING):
            down, up = reach.get(j, (0, 0))
            for way, far in ((1, up), (-1, down)):
                last, depth = j, 0
                for h in range(1, far + 1):
                    n = (j + way * h) % RING
                    if n in needed[j]:
                        depth += 1
                        self.edges[last].append((j, n, depth))
                        last = n


def make_plans():
    load = [0] * RING
    return [Plan(reach, visits, load) for reach, visits in GROUPS], load


PLANS, LOAD = make_plans()
SLOTS = max(len(p.slots[n]) for p in PLANS for n in range(RING))
GUESTS = max(len(p.guests[n]) for p in PLANS for n in range(RING))
EDGES = max(len(p.edges[n]) for p in PLANS for n in range(RING))
DEPTH = max(e[2] for p in PLANS for n in range(RING) for e in p.edges[n])
MERGE_LAG = 2
MIX_LAG = 4
AHEAD = 1


def relay_kernel(
    sections,
    rounds,
    up_ref,
    dqk_ref,
    dv_ref,
    upo_ref,
    dno_ref,
    own,
    kv,
    guest,
    note,
    reply,
    out,
    carr,
    kv_ssem,
    kv_rsem,
    q_ssem,
    q_rsem,
    o_ssem,
    o_rsem,
    ca_ssem,
    ca_rsem,
    swap_ssem,
    swap_rsem,
    back_ssem,
    back_rsem,
    own_sem,
    put_sem,
):
    half = ROWS // 2
    groups = len(GROUPS)
    width = groups * rounds * HD
    wide = groups * HD
    scale = LOG2E / math.sqrt(HD)
    s = lax.axis_index("section")
    r = lax.axis_index("replica")
    z = lax.axis_index("tensor")
    core = lax.rem(r, 2)
    twin = r + 1 - 2 * core

    def remote(src, dst, ssem, rsem, device):
        return pltpu.make_async_remote_copy(
            src_ref=src, dst_ref=dst, send_sem=ssem, recv_sem=rsem, device_id=device, device_id_type=MESH
        )

    def stage(part):
        return pltpu.make_async_copy(up_ref.at[:, pl.ds(part * width, width)], own.at[0, part], own_sem.at[part])

    for part in (1, 2, 0):
        stage(part).start()

    barrier = pltpu.get_barrier_semaphore()
    for d in range(1, RING):
        pl.semaphore_signal(barrier, inc=1, device_id={"tensor": lax.rem(z + d, RING)}, device_id_type=MESH)
    pl.semaphore_signal(barrier, inc=1, device_id={"replica": twin}, device_id_type=MESH)
    for step in (1, sections - 1):
        pl.semaphore_signal(
            barrier, inc=1, device_id={"section": lax.rem(s + step, sections)}, device_id_type=MESH
        )
    pl.semaphore_wait(barrier, RING - 1 + 1 + 2)

    my_rows = pl.ds(pl.multiple_of(core * half, half), half)

    def down_source(part, seq):
        if part < 2:
            return dqk_ref.at[seq, :, pl.ds(part * width, width)]
        return dv_ref.at[seq]

    def keep(part):
        return pltpu.make_async_copy(down_source(part, core), own.at[1, part, my_rows, :], own_sem.at[3 + part])

    def swap(part):
        return remote(
            down_source(part, 1 - core),
            own.at[1, part, my_rows, :],
            swap_ssem.at[part],
            swap_rsem.at[part],
            {"replica": twin},
        )

    for part in (1, 0, 2):
        keep(part).start()
        swap(part).start()
    for part in range(3):
        stage(part).wait()

    def lanes(group, t):
        return pl.ds(pl.multiple_of((t * groups + group) * HD, HD), HD)

    def round_lanes(t):
        return pl.ds(pl.multiple_of(t * wide, wide), wide)

    def parity_order(index):
        return 2 * lax.rem(index, half) + index // half

    key_row = lax.broadcasted_iota(jnp.int32, (ROWS, ROWS), 0)
    query_col = lax.broadcasted_iota(jnp.int32, (ROWS, ROWS), 1)

    def partial(queries, blocks, allowed):
        scores = []
        for keys, _, diagonal in blocks:
            score = lax.dot_general(
                keys, queries, (((1,), (1,)), ((), ())), preferred_element_type=jnp.float32
            )
            scores.append(jnp.where(allowed, score, -1e30) if diagonal else score)
        peak = functools.reduce(jnp.maximum, scores)
        peak = jnp.max(peak, axis=0, keepdims=True)
        weights = [jnp.exp2((score - peak) * scale) for score in scores]
        total = jnp.sum(functools.reduce(jnp.add, weights), axis=0, keepdims=True)
        mixed = None
        for weight, (_, values, _) in zip(weights, blocks):
            term = lax.dot_general(
                values,
                weight.astype(jnp.bfloat16),
                (((0,), (0,)), ((), ())),
                preferred_element_type=jnp.float32,
            )
            mixed = term if mixed is None else mixed + term
        return mixed / total, peak * scale + jnp.log2(total)

    def program(me):
        def kv_source(layer, group, j, kind, t):
            if j == me:
                return own.at[layer, 1 + kind, :, lanes(group, t)]
            return kv.at[layer, group, PLANS[group].slots[me].index(j), kind, t]

        def kv_copy(layer, group, edge, kind, t):
            j, n, _ = PLANS[group].edges[me][edge]
            slot = PLANS[group].slots[n].index(j)
            return remote(
                kv_source(layer, group, j, kind, t),
                kv.at[layer, group, slot, kind, t],
                kv_ssem.at[layer, group, edge, kind],
                kv_rsem.at[layer, group, slot, kind, t],
                {"tensor": n},
            )

        def kv_arrival(layer, group, slot, kind, t):
            place = kv.at[layer, group, slot, kind, t]
            return remote(
                place,
                place,
                kv_ssem.at[layer, group, 0, kind],
                kv_rsem.at[layer, group, slot, kind, t],
                {"tensor": (me + 1) % RING},
            )

        def q_copy(layer, group, t):
            n = PLANS[group].visits[me]
            slot = PLANS[group].guests[n].index(me)
            return remote(
                own.at[layer, 0, :, lanes(group, t)],
                guest.at[layer, group, slot, t],
                q_ssem.at[layer, group],
                q_rsem.at[layer, group, slot, t],
                {"tensor": n},
            )

        def q_arrival(layer, group, slot, t):
            place = guest.at[layer, group, slot, t]
            return remote(
                place,
                place,
                q_ssem.at[layer, group],
                q_rsem.at[layer, group, slot, t],
                {"tensor": (me + 1) % RING},
            )

        def o_copy(layer, group, slot, t):
            i = PLANS[group].guests[me][slot]
            return remote(
                note.at[layer, group, slot, t],
                reply.at[layer, group, t],
                o_ssem.at[layer, group, slot],
                o_rsem.at[layer, group, t],
                {"tensor": i},
            )

        def o_arrival(layer, group, t):
            place = reply.at[layer, group, t]
            return remote(
                place,
                place,
                o_ssem.at[layer, group, 0],
                o_rsem.at[layer, group, t],
                {"tensor": (me + 1) % RING},
            )

        def send_kv(layer, kind, t):
            for group, plan in enumerate(PLANS):
                for edge, (j, _, _) in enumerate(plan.edges[me]):
                    if j == me:
                        kv_copy(layer, group, edge, kind, t).start()

        def send_q(layer, t):
            for group, plan in enumerate(PLANS):
                if me in plan.visits:
                    q_copy(layer, group, t).start()

        def waited(group, j):
            return any(e[0] == j for e in PLANS[group].edges[me])

        def forward(layer, t, depth):
            for group, plan in enumerate(PLANS):
                done = set()
                for edge, (j, _, deep) in enumerate(plan.edges[me]):
                    if j != me and deep == depth:
                        for kind in range(2):
                            if j not in done:
                                kv_arrival(layer, group, plan.slots[me].index(j), kind, t).wait_recv()
                            kv_copy(layer, group, edge, kind, t).start()
                        done.add(j)

        def block(layer, group, j, t):
            if j == me:
                at_head = lanes(group, t)
                return own[layer, 1, :, at_head], own[layer, 2, :, at_head], False
            slot = PLANS[group].slots[me].index(j)
            return kv[layer, group, slot, 0, t], kv[layer, group, slot, 1, t], False

        def serve(layer, t):
            for group, plan in enumerate(PLANS):
                for slot, j in enumerate(plan.slots[me]):
                    if not waited(group, j):
                        for kind in range(2):
                            kv_arrival(layer, group, slot, kind, t).wait_recv()
                for slot, i in enumerate(plan.guests[me]):
                    q_arrival(layer, group, slot, t).wait_recv()
                    blocks = [block(layer, group, j, t) for j in plan.away[i]]
                    mixed, level = partial(guest[layer, group, slot, t], blocks, None)
                    note[layer, group, slot, t, pl.ds(0, HD), :] = mixed.astype(jnp.bfloat16)
                    first = level.astype(jnp.bfloat16).astype(jnp.float32)
                    rest = level - first
                    second = rest.astype(jnp.bfloat16).astype(jnp.float32)
                    third = rest - second
                    line = lax.broadcasted_iota(jnp.int32, (NOTE, ROWS), 0)
                    tail = jnp.where(
                        line == 0, first, jnp.where(line == 1, second, jnp.where(line == 2, third, 0.0))
                    )
                    note[layer, group, slot, t, pl.ds(HD, NOTE), :] = tail.astype(jnp.bfloat16)
                    o_copy(layer, group, slot, t).start()

        def merge(layer, t):
            place = jnp.where(layer == 1, parity_order(key_row), key_row)
            against = jnp.where(layer == 1, parity_order(query_col), query_col)
            allowed = place <= against
            for group, plan in enumerate(PLANS):
                at_head = lanes(group, t)
                blocks = [block(layer, group, j, t) for j in plan.home[me] if j != me]
                blocks.append((own[layer, 1, :, at_head], own[layer, 2, :, at_head], True))
                mixed, level = partial(own[layer, 0, :, at_head], blocks, allowed)
                if me in plan.visits:
                    o_arrival(layer, group, t).wait_recv()
                    other = reply[layer, group, t, pl.ds(0, HD), :].astype(jnp.float32)
                    tail = reply[layer, group, t, pl.ds(HD, NOTE), :].astype(jnp.float32)
                    other_level = tail[0:1] + tail[1:2] + tail[2:3]
                    top = jnp.maximum(level, other_level)
                    mine = jnp.exp2(level - top)
                    theirs = jnp.exp2(other_level - top)
                    mixed = (mixed * mine + other * theirs) / (mine + theirs)
                out[layer, :, at_head] = mixed.T.astype(jnp.bfloat16)

        def put_up(t):
            return pltpu.make_async_copy(
                out.at[0, :, round_lanes(t)], upo_ref.at[:, round_lanes(t)], put_sem.at[0]
            )

        def put_down(t):
            return pltpu.make_async_copy(
                out.at[1, my_rows, round_lanes(t)], dno_ref.at[core, :, round_lanes(t)], put_sem.at[1]
            )

        def carry_on(t):
            return remote(
                out.at[0, :, round_lanes(t)],
                carr.at[:, round_lanes(t)],
                ca_ssem.at[t],
                ca_rsem.at[t],
                {"section": lax.rem(s + 1, sections)},
            )

        other_rows = pl.ds(pl.multiple_of((1 - core) * half, half), half)

        def give_back(t):
            return remote(
                out.at[1, other_rows, round_lanes(t)],
                dno_ref.at[core, :, round_lanes(t)],
                back_ssem.at[t],
                back_rsem.at[t],
                {"replica": twin},
            )

        def given_back(t):
            return remote(
                out.at[1, other_rows, round_lanes(t)],
                dno_ref.at[1 - core, :, round_lanes(t)],
                back_ssem.at[t],
                back_rsem.at[t],
                {"replica": twin},
            )

        def mix(t):
            here = round_lanes(t)

            @pl.when(s > 0)
            def _():
                carry_on(t).wait_recv()
                reorder = jnp.where(query_col == parity_order(key_row), 1.0, 0.0).astype(jnp.bfloat16)
                moved = jnp.dot(reorder, carr[:, here], preferred_element_type=jnp.float32)
                own[1, 2, :, here] = (own[1, 2, :, here].astype(jnp.float32) + moved).astype(jnp.bfloat16)

        def early(t, c):
            for kind in range(2):
                send_kv(0, kind, t)
            send_q(0, t)
            return c

        lax.fori_loop(0, AHEAD, early, 0)
        for part in range(3):
            keep(part).wait()
            swap(part).wait_recv()

        total = 2 * rounds

        def body(step, c):
            g = step - (DEPTH - 1)

            def ranged(index, low, high, act):
                @pl.when(jnp.logical_and(index >= low, index < high))
                def _():
                    act(index)

            def mix_and_send(index):
                mix(index)
                send_kv(1, 1, index)

            ahead = g + DEPTH - 1 + AHEAD
            ranged(ahead, AHEAD, rounds, lambda i: early(i, 0))

            def keys_and_queries(index):
                send_kv(1, 0, index)
                send_q(1, index)

            ranged(ahead - rounds, 0, rounds, keys_and_queries)
            ranged(g - MIX_LAG, 0, rounds, mix_and_send)
            for depth in range(2, DEPTH + 1):
                ranged(
                    g + DEPTH + 1 - depth,
                    0,
                    total,
                    lambda i, depth=depth: forward(i // rounds, lax.rem(i, rounds), depth),
                )

            def finish(index):
                layer = index // rounds
                t = lax.rem(index, rounds)
                merge(layer, t)

                @pl.when(layer == 0)
                def _():
                    put_up(t).start()

                    @pl.when(s < sections - 1)
                    def _():
                        carry_on(t).start()

                    put_up(t).wait()

                @pl.when(layer == 1)
                def _():
                    give_back(t).start()
                    put_down(t).start()
                    put_down(t).wait()

            ranged(g - MERGE_LAG, 0, total, finish)
            ranged(g, 0, total, lambda i: serve(i // rounds, lax.rem(i, rounds)))
            return c

        lax.fori_loop(0, total + DEPTH - 1 + MERGE_LAG, body, 0)

        for layer in range(2):
            for group, plan in enumerate(PLANS):
                for edge in range(len(plan.edges[me])):
                    for kind in range(2):
                        n = plan.edges[me][edge][1]
                        sent = kv.at[layer, group, 0, kind]
                        remote(
                            sent,
                            sent,
                            kv_ssem.at[layer, group, edge, kind],
                            kv_rsem.at[layer, group, 0, kind, 0],
                            {"tensor": n},
                        ).wait_send()
                if me in plan.visits:
                    sent = guest.at[layer, group, 0]
                    remote(
                        sent,
                        sent,
                        q_ssem.at[layer, group],
                        q_rsem.at[layer, group, 0, 0],
                        {"tensor": plan.visits[me]},
                    ).wait_send()
                for slot, i in enumerate(plan.guests[me]):
                    sent = note.at[layer, group, slot]
                    remote(
                        sent,
                        sent,
                        o_ssem.at[layer, group, slot],
                        o_rsem.at[layer, group, 0],
                        {"tensor": i},
                    ).wait_send()

        def settle(t, c):
            give_back(t).wait_send()
            given_back(t).wait_recv()

            @pl.when(s < sections - 1)
            def _():
                carry_on(t).wait_send()

            return c

        lax.fori_loop(0, rounds, settle, 0)
        for part in range(3):
            swap(part).wait_send()

    for me in range(RING):
        pl.when(z == me)(functools.partial(program, me))


def per_device(sections, up_qkv, down_qk, down_values):
    rows = up_qkv.shape[2]
    width = up_qkv.shape[3] // 3
    half = rows // 2
    groups = len(GROUPS)
    rounds = width // HD // groups
    up = up_qkv.reshape(rows, 3 * width)
    dqk = jnp.swapaxes(down_qk.reshape(half, 2, 2 * width), 0, 1)
    dv = jnp.swapaxes(down_values.reshape(half, 2, width), 0, 1)
    hbm = pl.BlockSpec(memory_space=pl.ANY)
    dma = pltpu.SemaphoreType.DMA

    def vmem(*shape):
        return pltpu.VMEM(shape, jnp.bfloat16)

    up_out, down = pl.pallas_call(
        functools.partial(relay_kernel, sections, rounds),
        name="relay",
        out_shape=(
            jax.ShapeDtypeStruct((rows, width), jnp.bfloat16),
            jax.ShapeDtypeStruct((2, half, width), jnp.bfloat16),
        ),
        in_specs=[hbm, hbm, hbm],
        out_specs=(hbm, hbm),
        scratch_shapes=[
            vmem(2, 3, rows, width),
            vmem(2, groups, SLOTS, 2, rounds, rows, HD),
            vmem(2, groups, GUESTS, rounds, rows, HD),
            vmem(2, groups, GUESTS, rounds, HD + NOTE, rows),
            vmem(2, groups, rounds, HD + NOTE, rows),
            vmem(2, rows, width),
            vmem(rows, width),
            dma((2, groups, EDGES, 2)),
            dma((2, groups, SLOTS, 2, rounds)),
            dma((2, groups)),
            dma((2, groups, GUESTS, rounds)),
            dma((2, groups, GUESTS)),
            dma((2, groups, rounds)),
            dma((rounds,)),
            dma((rounds,)),
            dma((3,)),
            dma((3,)),
            dma((rounds,)),
            dma((rounds,)),
            dma((6,)),
            dma((2,)),
        ],
        compiler_params=pltpu.CompilerParams(
            collective_id=0, has_side_effects=True, vmem_limit_bytes=60 * 1024 * 1024
        ),
    )(up, dqk, dv)
    down_out = jnp.swapaxes(down, 0, 1)
    return (
        up_out.reshape(1, 1, rows, width),
        down_out.reshape(1, 1, half, 2, width),
    )


def solution(mesh):
    placed = (
        P("section", "replica", "tensor", None),
        P("section", "replica", "tensor", None, None),
        P("section", "replica", "tensor", None, None),
    )
    return jax.shard_map(
        functools.partial(per_device, mesh.shape["section"]),
        mesh=mesh,
        in_specs=placed,
        out_specs=(placed[0], placed[1]),
        check_vma=False,
    )
```

time: 360 us -> 186 us (0.52); the launches traced: 353 us -> 185 us
  waiting for transfers between devices: 182 us -> 0 us
  Pallas kernels: 0 us -> 174 us
  matrix products: 51.4 us -> 0 us
  local copies, waits for them, and re-layouts: 47.7 us -> 9.78 us
  blocking collectives: 34.5 us -> 0 us
  starting transfers between devices: 29.4 us -> 0 us
  loops' own time: 4.34 us -> 0 us
    pallas_call x0 -> x1, Pallas kernels: none -> 174 us  [per_device(): pl.pallas_call(functools.partial(relay_kernel, sections, rounds), name='r...]
    all_to_all x3 -> x0, waiting for transfers between devices: 162 us -> none  [the longest x1 72 us: per_device(): lax.all_to_all(stacked, ('replica', 'tensor'), split_axis=3, concat_axis=...]
    all_to_all x1 -> x0, blocking collectives: 34.5 us -> none  [per_device(): lax.all_to_all(up_heads_out, 'tensor', split_axis=0, concat_axis=1, tiled...]
    sub x6 -> x0, matrix products: 29.8 us -> none  [one_block(): expsum = jnp.exp(scores - row_peak)]
    dot_general x6 -> x0, matrix products: 21.6 us -> none  [one_block(): jnp.einsum('hqk,khd->qhd', weights, values, preferred_element_type=jnp.fl...]
    all_to_all x3 -> x0, starting transfers between devices: 21 us -> none  [the longest x1 10 us: per_device(): lax.all_to_all(stacked, ('replica', 'tensor'), split_axis=3, concat_axis=...]
    ppermute x2 -> x0, waiting for transfers between devices: 19.8 us -> none  [the longest x1 19.8 us: passed_along(): return lax.ppermute(array, axis, pairs)]
    reshape x5 -> x0, local copies, waits for them, and re-layouts: 10.4 us -> none  [the longest x1 3.7 us: per_device(): lax.map(one_group, grouped)]
  transfers between devices with their start and end apart: 5 -> 0, of which waited for: 4 -> 0; matrix products, arithmetic and copies ran while one was open for 2% -> 0% of each run, Pallas kernels for 0% -> 0%
where the time goes in v2:
time: 186 us; the launch traced here: 185 us
  Pallas kernels  174 us (94%)
  local copies, waits for them, and re-layouts  9.78 us (5%)
    pallas_call x1, Pallas kernels, per_device(): pl.pallas_call(functools.partial(relay_kernel, sections, rounds), name='r...  174 us
    unnamed x8, local copies, waits for them, and re-layouts  9.78 us

profile of v2, /device:TPU:225, one launch (start us, length us, event | category | flops | bytes accessed | tf_op | source)
XLA Modules:
  0.0 184.9 jit_solution(7079060148523482478)
XLA Ops:
  0.6 0.0 copy-start
  0.6 2.9 %copy.11 = bf16[1,1,64,2,4096]{4,2,3,1,0:T(8,128)(2,1)} copy(bf16[1,1,64,2,4096]{4,3,2,1,0:T(2,128)(2,1)} %param.5) | data formatting | bytes 2097152 | tf_op args[2]
  3.6 0.0 copy-done
  3.6 2.5 %copy.10 = bf16[1,1,64,2,8192]{4,2,3,1,0:T(8,128)(2,1)} copy(bf16[1,1,64,2,8192]{4,3,2,1,0:T(2,128)(2,1)S(1)} %copy-done) | data formatting | bytes 4194304 | tf_op args[1]
  6.1 174.5 %relay.1 = (bf16[128,4096]{1,0:T(8,128)(2,1)}, bf16[2,64,4096]{2,1,0:T(8,128)(2,1)}) custom-call(bf16[128,12288]{1,0:T(8,128)(2,1)} %bitcast.17, bf16[2,64,8192]{2,1,0:T(8,128)(2,1)} %bitcast.15, bf16[2,64,4096]{2,1,0:T(8,128)(2,1)} %bitcast.16), custom_call_target="tpu_custom_call" | custom-call | tf_op jit(solution)/shard_map/relay/pallas_call | solution.py:558
  180.5 0.0 copy-start.1
  180.5 3.4 %copy.7 = bf16[1,1,64,2,4096]{4,3,2,1,0:T(2,128)(2,1)} copy(bf16[1,1,64,2,4096]{4,2,3,1,0:T(8,128)(2,1)} %bitcast.19) | data formatting | bytes 2097152
  183.9 0.0 copy-done.1
  183.9 1.0 copy.13
Async XLA Ops:
  0.6 2.9 %copy-start = (bf16[1,1,64,2,8192]{4,3,2,1,0:T(2,128)(2,1)S(1)}, bf16[1,1,64,2,8192]{4,3,2,1,0:T(2,128)(2,1)}, u32[]{:S(2)}) copy-start(bf16[1,1,64,2,8192]{4,3,2,1,0:T(2,128)(2,1)} %param.4) | copy-start | bytes 6291460
  180.5 3.4 %copy-start.1 = (bf16[128,4096]{1,0:T(8,128)(2,1)S(1)}, bf16[128,4096]{1,0:T(8,128)(2,1)}, u32[]{:S(2)}) copy-start(bf16[128,4096]{1,0:T(8,128)(2,1)} %get-tuple-element.4) | copy-start | bytes 3145732

commit v3 on v2

--- a/solution.py
+++ b/solution.py
@@ -17,70 +17,49 @@
 
 GROUPS = (
     (
-        {0: (3, 1), 1: (4, 0), 2: (0, 2), 3: (0, 1), 5: (1, 0), 6: (0, 1)},
-        {2: 1, 3: 5, 4: 5, 5: 4, 6: 4, 7: 4},
+        ({0: (3, 1), 1: (4, 0), 2: (0, 2), 3: (0, 1), 5: (1, 0), 6: (0, 1)}, {2: (1,), 3: (5,), 4: (5,), 5: (4,), 6: (4,), 7: (4,)}),
     ),
     (
-        {0: (2, 1), 1: (3, 0), 2: (4, 0), 3: (0, 2), 4: (0, 1), 6: (1, 0)},
-        {2: 1, 3: 0, 4: 6, 5: 6, 6: 5, 7: 5},
+        ({0: (3, 1), 1: (4, 0), 2: (0, 2), 3: (0, 1), 5: (1, 0), 6: (0, 1)}, {2: (1,), 3: (5,), 4: (5,), 5: (4,), 6: (4,), 7: (4,)}),
+        ({0: (0, 2), 1: (1, 1), 2: (2, 0), 3: (3, 0), 4: (0, 2), 5: (0, 1)}, {3: (2,), 4: (2,), 5: (0,), 6: (0,), 7: (6, 0)}),
     ),
     (
-        {0: (0, 3), 1: (0, 2), 2: (0, 1), 3: (1, 0), 4: (2, 0), 5: (0, 2), 6: (0, 1)},
-        {4: 3, 5: 3, 6: 3, 7: 2},
+        ({0: (0, 3), 1: (0, 2), 2: (0, 1), 3: (1, 0), 4: (2, 0), 5: (0, 2), 6: (0, 1)}, {4: (3,), 5: (3,), 6: (3,), 7: (2,)}),
+        ({0: (0, 2), 1: (0, 1), 2: (1, 0), 3: (2, 0), 4: (0, 2), 5: (0, 1)}, {3: (2,), 4: (2,), 5: (2,), 6: (1,), 7: (6, 1)}),
     ),
     (
-        {0: (0, 2), 1: (0, 1), 2: (1, 0), 3: (2, 0), 4: (3, 0), 5: (0, 2), 6: (0, 1)},
-        {3: 2, 4: 2, 5: 2, 6: 1, 7: 1},
+        ({0: (0, 2), 1: (0, 1), 2: (1, 0), 3: (2, 0), 4: (3, 0), 5: (0, 1)}, {3: (2,), 4: (2,), 5: (2,), 6: (1,), 7: (6, 1)}),
+        ({0: (0, 1), 1: (1, 0), 2: (2, 0), 3: (3, 0), 4: (0, 1), 6: (1, 0)}, {2: (1,), 3: (1,), 4: (1,), 5: (0,), 6: (5, 0), 7: (5, 0)}),
     ),
 )
 
 
 class Plan:
-    def __init__(self, reach, visits, load):
+    def __init__(self, reach, visits, share, load):
         arcs = {}
         for j in range(RING):
             down, up = reach.get(j, (0, 0))
             arcs[j] = {(j + h) % RING for h in range(1, up + 1)} | {(j - h) % RING for h in range(1, down + 1)}
         needed = {j: set() for j in range(RING)}
-        home = {i: [i] for i in range(RING)}
-        away = {i: [] for i in range(RING)}
+        met = {i: {} for i in range(RING)}
         loose = []
         for i in range(RING):
-            load[i] += 1
+            load[i] += share
             for j in range(i):
-                spot = visits.get(i)
-                here = i in arcs[j]
-                there = spot is not None and (spot in arcs[j] or spot == j)
-                assert here or there, (i, j)
-                if here and there:
-                    loose.append((i, j))
-                elif here:
-                    home[i].append(j)
-                    needed[j].add(i)
-                    load[i] += 1
-                else:
-                    away[i].append(j)
-                    load[spot] += 1
-                    if spot != j:
-                        needed[j].add(spot)
-        for i, j in loose:
-            spot = visits[i]
-            extra_home = 0 if i in needed[j] else 8
-            extra_away = 0 if spot == j or spot in needed[j] else 8
-            if load[i] + extra_home <= load[spot] + extra_away:
-                home[i].append(j)
-                needed[j].add(i)
-                load[i] += 1
-            else:
-                away[i].append(j)
-                load[spot] += 1
-                if spot != j:
-                    needed[j].add(spot)
-        self.home = {i: sorted(home[i]) for i in home}
-        self.away = {i: sorted(away[i]) for i in away}
-        self.visits = {i: n for i, n in visits.items() if away[i]}
+                spots = [n for n in (i, *visits.get(i, ())) if n in arcs[j] or n == j]
+                assert spots, (i, j)
+                loose.append((len(spots), i, j, spots))
+        for _, i, j, spots in sorted(loose):
+            best = min(spots, key=lambda n: load[n] + (0 if n == j or n in needed[j] else 8))
+            met[i].setdefault(best, []).append(j)
+            load[best] += share
+            if best != j:
+                needed[j].add(best)
+        self.home = {i: sorted(met[i].get(i, [])) for i in range(RING)}
+        self.visits = {i: [n for n in visits.get(i, ()) if n in met[i]] for i in range(RING)}
+        self.away = {(i, n): sorted(met[i][n]) for i in range(RING) for n in self.visits[i]}
         self.slots = {n: [j for j in range(RING) if n in needed[j]] for n in range(RING)}
-        self.guests = {n: [i for i in range(RING) if self.visits.get(i) == n] for n in range(RING)}
+        self.guests = {n: [i for i in range(RING) if n in self.visits[i]] for n in range(RING)}
         self.edges = {n: [] for n in range(RING)}
         for j in range(RING):
             down, up = reach.get(j, (0, 0))
@@ -96,14 +75,16 @@
 
 def make_plans():
     load = [0] * RING
-    return [Plan(reach, visits, load) for reach, visits in GROUPS], load
+    return [[Plan(*table, 2 // len(tables), load) for table in tables] for tables in GROUPS], load
 
 
 PLANS, LOAD = make_plans()
-SLOTS = max(len(p.slots[n]) for p in PLANS for n in range(RING))
-GUESTS = max(len(p.guests[n]) for p in PLANS for n in range(RING))
-EDGES = max(len(p.edges[n]) for p in PLANS for n in range(RING))
-DEPTH = max(e[2] for p in PLANS for n in range(RING) for e in p.edges[n])
+ALL = [plan for plans in PLANS for plan in plans]
+SLOTS = max(len(p.slots[n]) for p in ALL for n in range(RING))
+GUESTS = max(len(p.guests[n]) for p in ALL for n in range(RING))
+EDGES = max(len(p.edges[n]) for p in ALL for n in range(RING))
+VISITS = max(len(p.visits[n]) for p in ALL for n in range(RING))
+DEPTH = max(e[2] for p in ALL for n in range(RING) for e in p.edges[n])
 MERGE_LAG = 2
 MIX_LAG = 4
 AHEAD = 1
@@ -231,114 +212,108 @@
         return mixed / total, peak * scale + jnp.log2(total)
 
     def program(me):
-        def kv_source(layer, group, j, kind, t):
+        def each(t, act):
+            for group, plans in enumerate(PLANS):
+                for turn, plan in enumerate(plans):
+                    todo = functools.partial(act, group, turn, plan)
+                    if len(plans) == 1:
+                        todo()
+                    else:
+                        pl.when(lax.rem(t, 2) == turn)(todo)
+
+        def kv_copy(layer, group, turn, plan, edge, kind, t):
+            j, n, _ = plan.edges[me][edge]
+            slot = plan.slots[n].index(j)
             if j == me:
-                return own.at[layer, 1 + kind, :, lanes(group, t)]
-            return kv.at[layer, group, PLANS[group].slots[me].index(j), kind, t]
-
-        def kv_copy(layer, group, edge, kind, t):
-            j, n, _ = PLANS[group].edges[me][edge]
-            slot = PLANS[group].slots[n].index(j)
+                source = own.at[layer, 1 + kind, :, lanes(group, t)]
+            else:
+                source = kv.at[layer, group, plan.slots[me].index(j), kind, t]
             return remote(
-                kv_source(layer, group, j, kind, t),
+                source,
                 kv.at[layer, group, slot, kind, t],
-                kv_ssem.at[layer, group, edge, kind],
+                kv_ssem.at[layer, group, turn, edge, kind],
                 kv_rsem.at[layer, group, slot, kind, t],
                 {"tensor": n},
             )
 
+        def arrival(place, sem):
+            return remote(place, place, put_sem.at[2], sem, {"tensor": (me + 1) % RING})
+
         def kv_arrival(layer, group, slot, kind, t):
-            place = kv.at[layer, group, slot, kind, t]
-            return remote(
-                place,
-                place,
-                kv_ssem.at[layer, group, 0, kind],
-                kv_rsem.at[layer, group, slot, kind, t],
-                {"tensor": (me + 1) % RING},
-            )
-
-        def q_copy(layer, group, t):
-            n = PLANS[group].visits[me]
-            slot = PLANS[group].guests[n].index(me)
+            return arrival(kv.at[layer, group, slot, kind, t], kv_rsem.at[layer, group, slot, kind, t])
+
+        def q_copy(layer, group, turn, plan, visit, t):
+            n = plan.visits[me][visit]
+            slot = plan.guests[n].index(me)
             return remote(
                 own.at[layer, 0, :, lanes(group, t)],
                 guest.at[layer, group, slot, t],
-                q_ssem.at[layer, group],
+                q_ssem.at[layer, group, turn, visit],
                 q_rsem.at[layer, group, slot, t],
                 {"tensor": n},
             )
 
         def q_arrival(layer, group, slot, t):
-            place = guest.at[layer, group, slot, t]
-            return remote(
-                place,
-                place,
-                q_ssem.at[layer, group],
-                q_rsem.at[layer, group, slot, t],
-                {"tensor": (me + 1) % RING},
-            )
-
-        def o_copy(layer, group, slot, t):
-            i = PLANS[group].guests[me][slot]
+            return arrival(guest.at[layer, group, slot, t], q_rsem.at[layer, group, slot, t])
+
+        def o_copy(layer, group, turn, plan, slot, t):
+            i = plan.guests[me][slot]
+            visit = plan.visits[i].index(me)
             return remote(
                 note.at[layer, group, slot, t],
-                reply.at[layer, group, t],
-                o_ssem.at[layer, group, slot],
-                o_rsem.at[layer, group, t],
+                reply.at[layer, group, visit, t],
+                o_ssem.at[layer, group, turn, slot],
+                o_rsem.at[layer, group, visit, t],
                 {"tensor": i},
             )
 
-        def o_arrival(layer, group, t):
-            place = reply.at[layer, group, t]
-            return remote(
-                place,
-                place,
-                o_ssem.at[layer, group, 0],
-                o_rsem.at[layer, group, t],
-                {"tensor": (me + 1) % RING},
-            )
+        def o_arrival(layer, group, visit, t):
+            return arrival(reply.at[layer, group, visit, t], o_rsem.at[layer, group, visit, t])
 
         def send_kv(layer, kind, t):
-            for group, plan in enumerate(PLANS):
+            def act(group, turn, plan):
                 for edge, (j, _, _) in enumerate(plan.edges[me]):
                     if j == me:
-                        kv_copy(layer, group, edge, kind, t).start()
+                        kv_copy(layer, group, turn, plan, edge, kind, t).start()
+
+            each(t, act)
 
         def send_q(layer, t):
-            for group, plan in enumerate(PLANS):
-                if me in plan.visits:
-                    q_copy(layer, group, t).start()
-
-        def waited(group, j):
-            return any(e[0] == j for e in PLANS[group].edges[me])
+            def act(group, turn, plan):
+                for visit in range(len(plan.visits[me])):
+                    q_copy(layer, group, turn, plan, visit, t).start()
+
+            each(t, act)
 
         def forward(layer, t, depth):
-            for group, plan in enumerate(PLANS):
+            def act(group, turn, plan):
                 done = set()
                 for edge, (j, _, deep) in enumerate(plan.edges[me]):
                     if j != me and deep == depth:
                         for kind in range(2):
                             if j not in done:
                                 kv_arrival(layer, group, plan.slots[me].index(j), kind, t).wait_recv()
-                            kv_copy(layer, group, edge, kind, t).start()
+                            kv_copy(layer, group, turn, plan, edge, kind, t).start()
                         done.add(j)
 
-        def block(layer, group, j, t):
+            each(t, act)
+
+        def block(layer, group, plan, j, t):
             if j == me:
                 at_head = lanes(group, t)
                 return own[layer, 1, :, at_head], own[layer, 2, :, at_head], False
-            slot = PLANS[group].slots[me].index(j)
+            slot = plan.slots[me].index(j)
             return kv[layer, group, slot, 0, t], kv[layer, group, slot, 1, t], False
 
         def serve(layer, t):
-            for group, plan in enumerate(PLANS):
+            def act(group, turn, plan):
                 for slot, j in enumerate(plan.slots[me]):
-                    if not waited(group, j):
+                    if not any(e[0] == j for e in plan.edges[me]):
                         for kind in range(2):
                             kv_arrival(layer, group, slot, kind, t).wait_recv()
                 for slot, i in enumerate(plan.guests[me]):
                     q_arrival(layer, group, slot, t).wait_recv()
-                    blocks = [block(layer, group, j, t) for j in plan.away[i]]
+                    blocks = [block(layer, group, plan, j, t) for j in plan.away[i, me]]
                     mixed, level = partial(guest[layer, group, slot, t], blocks, None)
                     note[layer, group, slot, t, pl.ds(0, HD), :] = mixed.astype(jnp.bfloat16)
                     first = level.astype(jnp.bfloat16).astype(jnp.float32)
@@ -350,27 +325,34 @@
                         line == 0, first, jnp.where(line == 1, second, jnp.where(line == 2, third, 0.0))
                     )
                     note[layer, group, slot, t, pl.ds(HD, NOTE), :] = tail.astype(jnp.bfloat16)
-                    o_copy(layer, group, slot, t).start()
+                    o_copy(layer, group, turn, plan, slot, t).start()
+
+            each(t, act)
 
         def merge(layer, t):
             place = jnp.where(layer == 1, parity_order(key_row), key_row)
             against = jnp.where(layer == 1, parity_order(query_col), query_col)
             allowed = place <= against
-            for group, plan in enumerate(PLANS):
+
+            def act(group, turn, plan):
                 at_head = lanes(group, t)
-                blocks = [block(layer, group, j, t) for j in plan.home[me] if j != me]
+                blocks = [block(layer, group, plan, j, t) for j in plan.home[me]]
                 blocks.append((own[layer, 1, :, at_head], own[layer, 2, :, at_head], True))
                 mixed, level = partial(own[layer, 0, :, at_head], blocks, allowed)
-                if me in plan.visits:
-                    o_arrival(layer, group, t).wait_recv()
-                    other = reply[layer, group, t, pl.ds(0, HD), :].astype(jnp.float32)
-                    tail = reply[layer, group, t, pl.ds(HD, NOTE), :].astype(jnp.float32)
-                    other_level = tail[0:1] + tail[1:2] + tail[2:3]
-                    top = jnp.maximum(level, other_level)
-                    mine = jnp.exp2(level - top)
-                    theirs = jnp.exp2(other_level - top)
-                    mixed = (mixed * mine + other * theirs) / (mine + theirs)
+                parts = [(mixed, level)]
+                for visit in range(len(plan.visits[me])):
+                    o_arrival(layer, group, visit, t).wait_recv()
+                    other = reply[layer, group, visit, t, pl.ds(0, HD), :].astype(jnp.float32)
+                    tail = reply[layer, group, visit, t, pl.ds(HD, NOTE), :].astype(jnp.float32)
+                    parts.append((other, tail[0:1] + tail[1:2] + tail[2:3]))
+                if len(parts) > 1:
+                    top = functools.reduce(jnp.maximum, [level for _, level in parts])
+                    shares = [jnp.exp2(level - top) for _, level in parts]
+                    weighed = [part * share for (part, _), share in zip(parts, shares)]
+                    mixed = functools.reduce(jnp.add, weighed) / functools.reduce(jnp.add, shares)
                 out[layer, :, at_head] = mixed.T.astype(jnp.bfloat16)
+
+            each(t, act)
 
         def put_up(t):
             return pltpu.make_async_copy(
@@ -490,37 +472,35 @@
 
         lax.fori_loop(0, total + DEPTH - 1 + MERGE_LAG, body, 0)
 
+        def sent(place, ssem, rsem, n):
+            remote(place, place, ssem, rsem, {"tensor": n}).wait_send()
+
         for layer in range(2):
-            for group, plan in enumerate(PLANS):
-                for edge in range(len(plan.edges[me])):
-                    for kind in range(2):
-                        n = plan.edges[me][edge][1]
-                        sent = kv.at[layer, group, 0, kind]
-                        remote(
-                            sent,
-                            sent,
-                            kv_ssem.at[layer, group, edge, kind],
-                            kv_rsem.at[layer, group, 0, kind, 0],
-                            {"tensor": n},
-                        ).wait_send()
-                if me in plan.visits:
-                    sent = guest.at[layer, group, 0]
-                    remote(
-                        sent,
-                        sent,
-                        q_ssem.at[layer, group],
-                        q_rsem.at[layer, group, 0, 0],
-                        {"tensor": plan.visits[me]},
-                    ).wait_send()
-                for slot, i in enumerate(plan.guests[me]):
-                    sent = note.at[layer, group, slot]
-                    remote(
-                        sent,
-                        sent,
-                        o_ssem.at[layer, group, slot],
-                        o_rsem.at[layer, group, 0],
-                        {"tensor": i},
-                    ).wait_send()
+            for group, plans in enumerate(PLANS):
+                turns = pl.ds(0, rounds // len(plans))
+                for turn, plan in enumerate(plans):
+                    for edge, (_, n, _) in enumerate(plan.edges[me]):
+                        for kind in range(2):
+                            sent(
+                                kv.at[layer, group, 0, kind, turns],
+                                kv_ssem.at[layer, group, turn, edge, kind],
+                                kv_rsem.at[layer, group, 0, kind, 0],
+                                n,
+                            )
+                    for visit, n in enumerate(plan.visits[me]):
+                        sent(
+                            guest.at[layer, group, 0, turns],
+                            q_ssem.at[layer, group, turn, visit],
+                            q_rsem.at[layer, group, 0, 0],
+                            n,
+                        )
+                    for slot, n in enumerate(plan.guests[me]):
+                        sent(
+                            note.at[layer, group, slot, turns],
+                            o_ssem.at[layer, group, turn, slot],
+                            o_rsem.at[layer, group, 0, 0],
+                            n,
+                        )
 
         def settle(t, c):
             give_back(t).wait_send()
@@ -569,15 +549,15 @@
             vmem(2, groups, SLOTS, 2, rounds, rows, HD),
             vmem(2, groups, GUESTS, rounds, rows, HD),
             vmem(2, groups, GUESTS, rounds, HD + NOTE, rows),
-            vmem(2, groups, rounds, HD + NOTE, rows),
+            vmem(2, groups, VISITS, rounds, HD + NOTE, rows),
             vmem(2, rows, width),
             vmem(rows, width),
-            dma((2, groups, EDGES, 2)),
+            dma((2, groups, 2, EDGES, 2)),
             dma((2, groups, SLOTS, 2, rounds)),
-            dma((2, groups)),
+            dma((2, groups, 2, VISITS)),
             dma((2, groups, GUESTS, rounds)),
-            dma((2, groups, GUESTS)),
-            dma((2, groups, rounds)),
+            dma((2, groups, 2, GUESTS)),
+            dma((2, groups, VISITS, rounds)),
             dma((rounds,)),
             dma((rounds,)),
             dma((3,)),
@@ -585,10 +565,10 @@
             dma((rounds,)),
             dma((rounds,)),
             dma((6,)),
-            dma((2,)),
+            dma((3,)),
         ],
         compiler_params=pltpu.CompilerParams(
-            collective_id=0, has_side_effects=True, vmem_limit_bytes=60 * 1024 * 1024
+            collective_id=0, has_side_effects=True, vmem_limit_bytes=46 * 1024 * 1024
         ),
     )(up, dqk, dv)
     down_out = jnp.swapaxes(down, 0, 1)

time: 186 us -> 181 us (0.973)
  local copies, waits for them, and re-layouts: 9.78 us -> 6.15 us
    unnamed x8 -> x6, local copies, waits for them, and re-layouts: 9.78 us -> 6.15 us
where the time goes in v3:
time: 181 us
  Pallas kernels  174 us (96%)
  local copies, waits for them, and re-layouts  6.15 us (3%)
    pallas_call x1, Pallas kernels, per_device(): pl.pallas_call(functools.partial(relay_kernel, sections, rounds), name='r...  174 us
    unnamed x6, local copies, waits for them, and re-layouts  6.15 us

profile of v3, /device:TPU:225, one launch (start us, length us, event | category | flops | bytes accessed | tf_op | source)
XLA Modules:
  0.0 180.9 jit_solution(4551962394800580846)
XLA Ops:
  0.6 0.0 copy-start
  0.6 2.0 %copy.11 = bf16[1,1,64,2,4096]{4,2,3,1,0:T(8,128)(2,1)S(1)} copy(bf16[1,1,64,2,4096]{4,3,2,1,0:T(2,128)(2,1)} %param.5) | data formatting | bytes 2097152 | tf_op args[2]
  2.6 0.0 copy-done
  2.6 1.2 copy.10
  3.8 174.1 %relay.1 = (bf16[128,4096]{1,0:T(8,128)(2,1)S(1)}, bf16[2,64,4096]{2,1,0:T(8,128)(2,1)S(1)}) custom-call(bf16[128,12288]{1,0:T(8,128)(2,1)} %bitcast.19, bf16[2,64,8192]{2,1,0:T(8,128)(2,1)S(1)} %bitcast.15, bf16[2,64,4096]{2,1,0:T(8,128)(2,1)S(1)} %bitcast.16), custom_call_target="tpu_custom_call" | custom-call | tf_op jit(solution)/shard_map/relay/pallas_call | solution.py:538
  177.9 2.1 %copy.7 = bf16[1,1,64,2,4096]{4,3,2,1,0:T(2,128)(2,1)} copy(bf16[1,1,64,2,4096]{4,2,3,1,0:T(8,128)(2,1)S(1)} %bitcast.18) | data formatting | bytes 2097152
  180.0 1.0 copy.13
Async XLA Ops:
  0.6 2.0 %copy-start = (bf16[1,1,64,2,8192]{4,3,2,1,0:T(2,128)(2,1)S(1)}, bf16[1,1,64,2,8192]{4,3,2,1,0:T(2,128)(2,1)}, u32[]{:S(2)}) copy-start(bf16[1,1,64,2,8192]{4,3,2,1,0:T(2,128)(2,1)} %param.4) | copy-start | bytes 6291460

commit v4 on v3

--- a/solution.py
+++ b/solution.py
@@ -105,6 +105,8 @@
     reply,
     out,
     carr,
+    raw,
+    split,
     kv_ssem,
     kv_rsem,
     q_ssem,
@@ -139,8 +141,13 @@
     def stage(part):
         return pltpu.make_async_copy(up_ref.at[:, pl.ds(part * width, width)], own.at[0, part], own_sem.at[part])
 
+    def fetch(part):
+        source = dv_ref if part == 2 else dqk_ref.at[:, :, pl.ds(part * width, width)]
+        return pltpu.make_async_copy(source, raw, own_sem.at[3])
+
     for part in (1, 2, 0):
         stage(part).start()
+    fetch(1).start()
 
     barrier = pltpu.get_barrier_semaphore()
     for d in range(1, RING):
@@ -154,26 +161,15 @@
 
     my_rows = pl.ds(pl.multiple_of(core * half, half), half)
 
-    def down_source(part, seq):
-        if part < 2:
-            return dqk_ref.at[seq, :, pl.ds(part * width, width)]
-        return dv_ref.at[seq]
-
-    def keep(part):
-        return pltpu.make_async_copy(down_source(part, core), own.at[1, part, my_rows, :], own_sem.at[3 + part])
-
     def swap(part):
         return remote(
-            down_source(part, 1 - core),
+            split.at[part],
             own.at[1, part, my_rows, :],
             swap_ssem.at[part],
             swap_rsem.at[part],
             {"replica": twin},
         )
 
-    for part in (1, 0, 2):
-        keep(part).start()
-        swap(part).start()
     for part in range(3):
         stage(part).wait()
 
@@ -188,6 +184,28 @@
 
     key_row = lax.broadcasted_iota(jnp.int32, (ROWS, ROWS), 0)
     query_col = lax.broadcasted_iota(jnp.int32, (ROWS, ROWS), 1)
+
+    def unzip(part, following):
+        fetch(part).wait()
+        seq = jnp.where(key_row < half, core, 1 - core)
+        apart = jnp.where(query_col == 2 * lax.rem(key_row, half) + seq, 1.0, 0.0).astype(jnp.bfloat16)
+
+        def piece(t, c):
+            here = round_lanes(t)
+            both = raw[:, :, here].reshape(ROWS, wide)
+            moved = jnp.dot(apart, both, preferred_element_type=jnp.float32).astype(jnp.bfloat16)
+            own[1, part, my_rows, here] = moved[:half]
+            split[part, :, here] = moved[half:]
+            return c
+
+        lax.fori_loop(0, rounds, piece, 0)
+        if following is not None:
+            fetch(following).start()
+        swap(part).start()
+
+    def swapped():
+        for part in range(3):
+            swap(part).wait_recv()
 
     def partial(queries, blocks, allowed):
         scores = []
@@ -410,14 +428,15 @@
             return c
 
         lax.fori_loop(0, AHEAD, early, 0)
-        for part in range(3):
-            keep(part).wait()
-            swap(part).wait_recv()
 
         total = 2 * rounds
 
         def body(step, c):
             g = step - (DEPTH - 1)
+            order = (1, 0, 2, None)
+            for turn in range(3):
+                pl.when(step == turn)(functools.partial(unzip, order[turn], order[turn + 1]))
+            pl.when(step == 5)(swapped)
 
             def ranged(index, low, high, act):
                 @pl.when(jnp.logical_and(index >= low, index < high))
@@ -527,8 +546,8 @@
     groups = len(GROUPS)
     rounds = width // HD // groups
     up = up_qkv.reshape(rows, 3 * width)
-    dqk = jnp.swapaxes(down_qk.reshape(half, 2, 2 * width), 0, 1)
-    dv = jnp.swapaxes(down_values.reshape(half, 2, width), 0, 1)
+    dqk = down_qk.reshape(half, 2, 2 * width)
+    dv = down_values.reshape(half, 2, width)
     hbm = pl.BlockSpec(memory_space=pl.ANY)
     dma = pltpu.SemaphoreType.DMA
 
@@ -552,6 +571,8 @@
             vmem(2, groups, VISITS, rounds, HD + NOTE, rows),
             vmem(2, rows, width),
             vmem(rows, width),
+            vmem(half, 2, width),
+            vmem(3, half, width),
             dma((2, groups, 2, EDGES, 2)),
             dma((2, groups, SLOTS, 2, rounds)),
             dma((2, groups, 2, VISITS)),
@@ -564,11 +585,11 @@
             dma((3,)),
             dma((rounds,)),
             dma((rounds,)),
-            dma((6,)),
+            dma((4,)),
             dma((3,)),
         ],
         compiler_params=pltpu.CompilerParams(
-            collective_id=0, has_side_effects=True, vmem_limit_bytes=46 * 1024 * 1024
+            collective_id=0, has_side_effects=True, vmem_limit_bytes=49 * 1024 * 1024
         ),
     )(up, dqk, dv)
     down_out = jnp.swapaxes(down, 0, 1)

time: 181 us -> 178 us (0.983)
  local copies, waits for them, and re-layouts: 6.15 us -> 4.25 us
    unnamed x6 -> x4, local copies, waits for them, and re-layouts: 6.15 us -> 4.25 us
where the time goes in v4:
time: 178 us; the launch traced here: 177 us
  Pallas kernels  173 us (97%)
  local copies, waits for them, and re-layouts  4.25 us (2%)
    pallas_call x1, Pallas kernels, per_device(): pl.pallas_call(functools.partial(relay_kernel, sections, rounds), name='r...  173 us
    unnamed x4, local copies, waits for them, and re-layouts  4.25 us

profile of v4, /device:TPU:225, one launch (start us, length us, event | category | flops | bytes accessed | tf_op | source)
XLA Modules:
  0.0 177.5 jit_solution(8359790298994315915)
XLA Ops:
  0.6 0.0 copy-start
  0.6 1.2 copy-done
  1.9 172.6 %relay.1 = (bf16[128,4096]{1,0:T(8,128)(2,1)S(1)}, bf16[2,64,4096]{2,1,0:T(8,128)(2,1)S(1)}) custom-call(bf16[128,12288]{1,0:T(8,128)(2,1)} %bitcast.10, bf16[64,2,8192]{2,1,0:T(2,128)(2,1)} %bitcast.11, bf16[64,2,4096]{2,1,0:T(2,128)(2,1)S(1)} %bitcast.9), custom_call_target="tpu_custom_call" | custom-call | tf_op jit(solution)/shard_map/relay/pallas_call | solution.py:557
  174.4 2.1 %copy.5 = bf16[1,1,64,2,4096]{4,3,2,1,0:T(2,128)(2,1)} copy(bf16[1,1,64,2,4096]{4,2,3,1,0:T(8,128)(2,1)S(1)} %bitcast.8) | data formatting | bytes 2097152
  176.5 1.0 copy.7
Async XLA Ops:
  0.6 1.2 copy-start

commit v5 on v4

--- a/solution.py
+++ b/solution.py
@@ -433,10 +433,7 @@
 
         def body(step, c):
             g = step - (DEPTH - 1)
-            order = (1, 0, 2, None)
-            for turn in range(3):
-                pl.when(step == turn)(functools.partial(unzip, order[turn], order[turn + 1]))
-            pl.when(step == 5)(swapped)
+            pl.when(step == 6)(swapped)
 
             def ranged(index, low, high, act):
                 @pl.when(jnp.logical_and(index >= low, index < high))
@@ -463,6 +460,10 @@
                     total,
                     lambda i, depth=depth: forward(i // rounds, lax.rem(i, rounds), depth),
                 )
+
+            order = (1, 0, 2, None)
+            for turn in range(3):
+                pl.when(step == turn + 2)(functools.partial(unzip, order[turn], order[turn + 1]))
 
             def finish(index):
                 layer = index // rounds

time: 178 us -> 179 us (level)
  no operation moved by 1% of the time
where the time goes in v5:
time: 179 us
  Pallas kernels  174 us (97%)
  local copies, waits for them, and re-layouts  4.25 us (2%)
    pallas_call x1, Pallas kernels, per_device(): pl.pallas_call(functools.partial(relay_kernel, sections, rounds), name='r...  174 us
    unnamed x4, local copies, waits for them, and re-layouts  4.25 us

profile of v5, /device:TPU:225, one launch (start us, length us, event | category | flops | bytes accessed | tf_op | source)
XLA Modules:
  0.0 178.6 jit_solution(11410491720918627608)
XLA Ops:
  0.6 0.0 copy-start
  0.6 1.2 copy-done
  1.9 173.7 %relay.1 = (bf16[128,4096]{1,0:T(8,128)(2,1)S(1)}, bf16[2,64,4096]{2,1,0:T(8,128)(2,1)S(1)}) custom-call(bf16[128,12288]{1,0:T(8,128)(2,1)} %bitcast.10, bf16[64,2,8192]{2,1,0:T(2,128)(2,1)} %bitcast.11, bf16[64,2,4096]{2,1,0:T(2,128)(2,1)S(1)} %bitcast.9), custom_call_target="tpu_custom_call" | custom-call | tf_op jit(solution)/shard_map/relay/pallas_call | solution.py:558
  175.5 2.1 %copy.5 = bf16[1,1,64,2,4096]{4,3,2,1,0:T(2,128)(2,1)} copy(bf16[1,1,64,2,4096]{4,2,3,1,0:T(8,128)(2,1)S(1)} %bitcast.8) | data formatting | bytes 2097152
  177.6 1.0 copy.7
Async XLA Ops:
  0.6 1.2 copy-start
